TPU v7x, 32 devices: a whole 2x2x4 slice. The times are simulated.
32 devices in a mesh: real: 2 (over x), space: 8 (over z, y), sub: 2 (over core).
Axes of the slice: x: 2, y: 2, z: 4, core: 2. Of those that a mesh axis runs over, the one named last changes fastest.
Arguments:
- force: float32 [4096, 384], P(('real', 'space')), parts along dimension 0, may hold values from -12 to 12
- drag: float32 [4096, 384], P(('real', 'space')), parts along dimension 0, may hold values from 0.5 to 2
- mode_matrix: float32 [6, 6], replicated, may hold values from -0.4 to 3, as said below
- tile_rows: int32 [8192], P(('real', 'space', 'sub')), parts along dimension 0, may hold values from 0 to 255
- tile_cols: int32 [8192], P(('real', 'space', 'sub')), parts along dimension 0, may hold values from 0 to 287
- gaps: bfloat16 [8192, 4096], P(('real', 'space', 'sub')), parts along dimension 0, may hold values from 0.0099487305 to 1
- send_blocks: int32 [16, 8, 4], P(('real', 'space')), parts along dimension 0, may hold values from 0 to 255
Outputs:
- velocity: float32 [4096, 384], P(('real', 'space')), parts along dimension 0
- residual: float32 [4096, 384], P(('real', 'space')), parts along dimension 0
There are 2 independent parts, one for each index of `real`. A program takes and returns all parts, laid end to end along the dimension named above; an argument that names none is the same for every part. Nothing has to cross between parts.
Inputs may be any that keep to these rules, and one draw needn't show every extreme that they name: `mode_matrix`: symmetric; every diagonal entry exceeds the sum of magnitudes of the other entries of its row.
All inputs are finite; a program needn't handle non-finite values.
Results may differ from a plain program's by a relative error of at most 0.0003.
Values sent between devices are 32-bit elements; how exact they have to be, the bound alone decides.
A program may use at most 64 MiB of HBM per device.

v0:
```python
import jax
import jax.numpy as jnp
from jax import lax
from jax.sharding import PartitionSpec as P

BLOCK = 64
ITERS = 2


coupling = 0.000244140625
gap_shift = 0.05


def shards(force, drag, mode_matrix, tile_rows, tile_cols, gaps, send_blocks):
    nspace = lax.axis_size("space")
    blocks = force.shape[0]
    width = force.shape[1]
    tiles_here = tile_rows.shape[0]
    slots = send_blocks.shape[2]
    halo_count = nspace * slots
    coeff = coupling / (gaps.astype(jnp.float32).reshape(tiles_here, BLOCK, BLOCK) + gap_shift)
    row_sums = jnp.sum(coeff, axis=2)
    col_sums = jnp.sum(coeff, axis=1)
    targets = jnp.arange(blocks + halo_count, dtype=jnp.int32)[:, None]
    row_onehot = (tile_rows[None, :] == targets).astype(jnp.float32)
    col_onehot = (tile_cols[None, :] == targets).astype(jnp.float32)
    exports = send_blocks.reshape(halo_count)
    own_targets = jnp.arange(blocks, dtype=jnp.int32)[:, None]
    return_onehot = (exports[None, :] == own_targets).astype(jnp.float32)
    highest = lax.Precision.HIGHEST

    def squares(vector):
        return lax.psum(jnp.sum(vector * vector), "space")

    velocity = jnp.zeros_like(force)
    residual = force
    direction = force
    norm_now = squares(residual)
    for step in range(ITERS):
        outgoing = jnp.take(direction, exports, axis=0).reshape(nspace, slots, width)
        incoming = lax.all_to_all(outgoing, "space", split_axis=0, concat_axis=0, tiled=True)
        joined = jnp.concatenate([direction, incoming.reshape(halo_count, width)], axis=0)
        row_vals = jnp.take(joined, tile_rows, axis=0).reshape(tiles_here, 6, BLOCK)
        col_vals = jnp.take(joined, tile_cols, axis=0).reshape(tiles_here, 6, BLOCK)
        row_part = row_sums[:, None, :] * row_vals - jnp.einsum(
            "tpq,tdq->tdp", coeff, col_vals, precision=highest
        )
        col_part = col_sums[:, None, :] * col_vals - jnp.einsum(
            "tpq,tdp->tdq", coeff, row_vals, precision=highest
        )
        summed = jnp.dot(
            row_onehot,
            row_part.reshape(tiles_here, width),
            precision=highest,
            preferred_element_type=jnp.float32,
        )
        summed = summed + jnp.dot(
            col_onehot,
            col_part.reshape(tiles_here, width),
            precision=highest,
            preferred_element_type=jnp.float32,
        )
        owned = summed[:blocks]
        halo_terms = summed[blocks:].reshape(nspace, slots, width)
        returned = lax.all_to_all(halo_terms, "space", split_axis=0, concat_axis=0, tiled=True)
        owned = owned + jnp.dot(
            return_onehot,
            returned.reshape(halo_count, width),
            precision=highest,
            preferred_element_type=jnp.float32,
        )
        pairs = lax.psum(owned, "sub")
        mixed = jnp.einsum(
            "ij,bjp->bip", mode_matrix, pairs.reshape(blocks, 6, BLOCK), precision=highest
        )
        image = drag * direction + mixed.reshape(blocks, width)
        alpha = norm_now / lax.psum(jnp.sum(direction * image), "space")
        velocity = velocity + alpha * direction
        residual = residual - alpha * image
        norm_next = squares(residual)
        direction = residual + norm_next / norm_now * direction
        norm_now = norm_next
    return (velocity, residual)


def solution(mesh):
    return jax.shard_map(
        shards,
        mesh=mesh,
        in_specs=(
            P(("real", "space"), None),
            P(("real", "space"), None),
            P(),
            P(("real", "space", "sub")),
            P(("real", "space", "sub")),
            P(("real", "space", "sub"), None),
            P(("real", "space"), None, None),
        ),
        out_specs=(P(("real", "space"), None), P(("real", "space"), None)),
        check_vma=False,
    )
```

profile of v0, /device:TPU:0, one launch (start us, length us, event | category | flops | bytes accessed | tf_op | source)
XLA Modules:
  0.0 259.2 jit_solution(774711100903316643)
XLA Ops:
  9.2 1.6 gather_fusion
  11.5 7.3 %all-to-all-start = ((f32[8,4,384]{2,1,0:T(4,128)}), f32[8,4,384]{2,1,0:T(4,128)S(1)}, u32[]{:S(2)}, u32[]{:S(2)}) async-start(f32[8,4,384]{2,1,0:T(4,128)} %reshape.88), calls=%async_computation | async-start | bytes 98304 | tf_op jit(solution)/shard_map/all_to_all | solution.py:41
  22.6 3.3 %copy.42 = bf16[256,4096]{0,1:T(8,128)(2,1)S(1)} copy(bf16[256,4096]{1,0:T(8,128)(2,1)} %param.16) | data formatting | bytes 4194304 | tf_op args[5]
  26.7 2.5 add_divide_fusion
  30.0 9.1 %copy.49 = f32[256,64,64]{2,1,0:T(8,128)} copy(f32[256,64,64]{0,2,1:T(8,128)} %bitcast.39) | data formatting | bytes 8388608 | tf_op jit(solution)/shard_map/div | solution.py:21
  39.2 2.4 reduce_sum.56
  45.8 9.6 %convolution_subtract_fusion.2 = f32[256,6,64]{2,1,0:T(8,128)S(1)} fusion(f32[256,6,64]{2,1,0:T(8,128)S(1)} %copy.46, f32[256,64,64]{2,1,0:T(8,128)} %copy.49, f32[256,6,64]{2,1,0:T(8,128)S(1)} %copy.48, f32[256,64]{1,0:T(8,128)} %copy.51), kind=kOutput, calls=%fused_computation.9 | convolution fusion | flops 75694080 | bytes 5439488 | tf_op jit(solution)/shard_map/tpq,tdp->tdq/dot_general | solution.py:48
  55.4 16.5 %convolution_subtract_fusion.3 = f32[256,6,64]{2,1,0:T(8,128)} fusion(f32[256,6,64]{2,1,0:T(8,128)S(1)} %copy.48, f32[256,64,64]{2,1,0:T(8,128)} %copy.49, f32[256,6,64]{2,1,0:T(8,128)S(1)} %copy.46, f32[256,64]{1,0:T(8,128)S(1)} %copy-done.4), kind=kOutput, calls=%fused_computation.10 | convolution fusion | flops 75694080 | bytes 5439488 | tf_op jit(solution)/shard_map/tpq,tdq->tdp/dot_general | solution.py:45
  72.0 1.5 copy.50
  74.7 12.5 %all_to_all.20 = f32[8,4,384]{2,1,0:T(4,128)S(1)} all-to-all(f32[8,4,384]{2,1,0:T(4,128)S(1)} %reshape.94), channel_id=1, replica_groups=mesh['real'=2,'space'=8,'sub'=2] {'space'}, dimensions={0} | all-to-all | bytes 98304 | tf_op jit(solution)/shard_map/all_to_all | solution.py:65
  89.0 16.3 %all-reduce.4.cloned.1.call-done = f32[256,6,64]{0,1,2:T(8,128)} async-done(((f32[256,6,64]{0,1,2:T(8,128)}), f32[256,6,64]{0,1,2:T(8,128)}) %all-reduce.4.cloned.1.call-update) | async-done | bytes 393232 | tf_op jit(solution)/shard_map/psum | solution.py:72
  105.2 1.6 convolution_bitcast_fusion.1
  107.9 22.3 %all-reduce = (f32[]{:T(128)}, f32[]{:T(128)}) all-reduce(f32[]{:T(128)} %get-tuple-element.5, f32[]{:T(128)} %get-tuple-element.4), channel_id=1, replica_groups=mesh['real'=2,'space'=8,'sub'=2] {'space'}, use_global_device_ids=true, to_apply=%region_1.0 | all-reduce | flops 2 | bytes 16 | tf_op jit(solution)/shard_map/psum | solution.py:33
  132.2 17.8 %psum.45 = f32[]{:T(128)} all-reduce(f32[]{:T(128)} %get-tuple-element.8), channel_id=1, replica_groups=mesh['real'=2,'space'=8,'sub'=2] {'space'}, use_global_device_ids=true, to_apply=%region_8.11 | all-reduce | flops 1 | bytes 8 | tf_op jit(solution)/shard_map/psum | solution.py:33
  152.3 9.9 %all_to_all.21 = f32[8,4,384]{2,1,0:T(4,128)S(1)} all-to-all(f32[8,4,384]{2,1,0:T(4,128)S(1)} %reshape.98), channel_id=1, replica_groups=mesh['real'=2,'space'=8,'sub'=2] {'space'}, dimensions={0} | all-to-all | bytes 98304 | tf_op jit(solution)/shard_map/all_to_all | solution.py:41
  166.1 1.4 copy.63
  167.5 10.4 %convolution_subtract_fusion = f32[256,6,64]{2,1,0:T(8,128)} fusion(f32[256,6,64]{2,1,0:T(8,128)S(1)} %copy.61, f32[256,64,64]{2,1,0:T(8,128)} %copy.49, f32[256,6,64]{2,1,0:T(8,128)S(1)} %copy.63, f32[256,64]{1,0:T(8,128)S(1)} %copy-done.6), kind=kOutput, calls=%fused_computation.7 | convolution fusion | flops 75694080 | bytes 5439488 | tf_op jit(solution)/shard_map/tpq,tdp->tdq/dot_general | solution.py:48
  177.9 16.3 %convolution_subtract_fusion.1 = f32[256,6,64]{2,1,0:T(8,128)} fusion(f32[256,6,64]{2,1,0:T(8,128)S(1)} %copy.63, f32[256,64,64]{2,1,0:T(8,128)} %copy.49, f32[256,6,64]{2,1,0:T(8,128)S(1)} %copy.61, f32[256,64]{1,0:T(8,128)S(1)} %copy-done.5), kind=kOutput, calls=%fused_computation.8 | convolution fusion | flops 75694080 | bytes 5439488 | tf_op jit(solution)/shard_map/tpq,tdq->tdp/dot_general | solution.py:45
  194.2 1.5 copy.65
  195.7 1.5 copy.69
  198.1 9.2 %all_to_all.22 = f32[8,4,384]{2,1,0:T(4,128)S(1)} all-to-all(f32[8,4,384]{2,1,0:T(4,128)S(1)} %reshape.104), channel_id=1, replica_groups=mesh['real'=2,'space'=8,'sub'=2] {'space'}, dimensions={0} | all-to-all | bytes 98304 | tf_op jit(solution)/shard_map/all_to_all | solution.py:65
  208.8 16.3 %all-reduce.6.cloned.1.call-done = f32[256,6,64]{0,1,2:T(8,128)} async-done(((f32[256,6,64]{0,1,2:T(8,128)}), f32[256,6,64]{0,1,2:T(8,128)}) %all-reduce.6.cloned.1.call-update) | async-done | bytes 393232 | tf_op jit(solution)/shard_map/psum | solution.py:72
  225.1 1.6 convolution_bitcast_fusion
  227.8 22.2 %psum.47 = f32[]{:T(128)} all-reduce(f32[]{:T(128)} %multiply_reduce_fusion), channel_id=1, replica_groups=mesh['real'=2,'space'=8,'sub'=2] {'space'}, use_global_device_ids=true, to_apply=%region_11.14 | all-reduce | flops 1 | bytes 8 | tf_op jit(solution)/shard_map/psum | solution.py:77
  (107 shorter events, 25.9 us)
Async XLA Ops:
  7.2 98.1 %copy-start = (f32[6,6]{1,0:T(8,128)S(1)}, f32[6,6]{1,0:T(8,128)}, u32[]{:S(2)}) copy-start(f32[6,6]{1,0:T(8,128)} %param.13) | copy-start | bytes 436
  8.0 0.5 copy-start.11
  8.0 3.5 %copy-start.13 = (pred[32]{0:T(512)(128)(4,1)}, pred[32]{0:T(512)(128)(4,1)S(1)}, u32[]{:S(2)}) copy-start(pred[32]{0:T(512)(128)(4,1)S(1)} %compare_and_fusion.2) | copy-start | bytes 100
  8.6 0.6 copy-start.10
  11.5 30.9 %all-to-all-start = ((f32[8,4,384]{2,1,0:T(4,128)}), f32[8,4,384]{2,1,0:T(4,128)S(1)}, u32[]{:S(2)}, u32[]{:S(2)}) async-start(f32[8,4,384]{2,1,0:T(4,128)} %reshape.88), calls=%async_computation | async-start | bytes 98304 | tf_op jit(solution)/shard_map/all_to_all | solution.py:41
  18.8 86.5 %all-reduce.4.cloned.1.call-start = ((), (), s32[]{:S(2)}) async-start(), calls=%async_computation.4 | async-start | bytes 1048576 | tf_op jit(solution)/shard_map/psum | solution.py:72
  19.5 24.9 %copy-start.17 = (pred[256]{0:T(512)(128)(4,1)}, pred[256]{0:T(512)(128)(4,1)S(1)}, u32[]{:S(2)}) copy-start(pred[256]{0:T(512)(128)(4,1)S(1)} %compare_and_fusion.1) | copy-start | bytes 772
  20.9 23.8 %copy-start.15 = (pred[256]{0:T(512)(128)(4,1)}, pred[256]{0:T(512)(128)(4,1)S(1)}, u32[]{:S(2)}) copy-start(pred[256]{0:T(512)(128)(4,1)S(1)} %compare_and_fusion) | copy-start | bytes 772
  42.4 1.0 copy-start.9
  45.8 9.6 %copy-start.4 = (f32[256,64]{1,0:T(8,128)S(1)}, f32[256,64]{1,0:T(8,128)}, u32[]{:S(2)}) copy-start(f32[256,64]{1,0:T(8,128)} %copy.43) | copy-start | bytes 196612
  55.4 18.4 %copy-start.7 = (s32[256]{0:T(256)S(1)}, s32[256]{0:T(256)}, u32[]{:S(2)}) copy-start(s32[256]{0:T(256)} %param.14) | copy-start | bytes 3076
  55.4 18.8 %copy-start.8 = (s32[256]{0:T(256)S(1)}, s32[256]{0:T(256)}, u32[]{:S(2)}) copy-start(s32[256]{0:T(256)} %param.15) | copy-start | bytes 3076
  72.0 15.3 %copy-start.12 = (s32[32]{0:T(128)S(1)}, s32[32]{0:T(128)}, u32[]{:S(2)}) copy-start(s32[32]{0:T(128)} %copy-done.11) | copy-start | bytes 388
  73.8 33.4 %copy-start.1 = (f32[256,384]{1,0:T(8,128)S(1)}, f32[256,384]{1,0:T(8,128)}, u32[]{:S(2)}) copy-start(f32[256,384]{1,0:T(8,128)} %param.11) | copy-start | bytes 1179652
  73.8 33.4 %copy-start.2 = (f32[256,384]{1,0:T(8,128)S(1)}, f32[256,384]{1,0:T(8,128)}, u32[]{:S(2)}) copy-start(f32[256,384]{1,0:T(8,128)} %param.12) | copy-start | bytes 1179652
  87.8 64.4 %copy-start.14 = (pred[32]{0:T(512)(128)(4,1)S(1)}, pred[32]{0:T(512)(128)(4,1)}, u32[]{:S(2)}) copy-start(pred[32]{0:T(512)(128)(4,1)} %copy-done.13) | copy-start | bytes 100
  88.9 136.2 %all-reduce.6.cloned.1.call-start = ((), (), s32[]{:S(2)}) async-start(), calls=%async_computation.5 | async-start | bytes 1048576 | tf_op jit(solution)/shard_map/psum | solution.py:72
  152.2 12.2 %copy-start.18 = (pred[256]{0:T(512)(128)(4,1)S(1)}, pred[256]{0:T(512)(128)(4,1)}, u32[]{:S(2)}) copy-start(pred[256]{0:T(512)(128)(4,1)} %copy-done.17) | copy-start | bytes 772
  162.2 2.3 copy-start.16
  163.3 4.2 %copy-start.6 = (f32[256,64]{1,0:T(8,128)S(1)}, f32[256,64]{1,0:T(8,128)}, u32[]{:S(2)}) copy-start(f32[256,64]{1,0:T(8,128)} %copy.51) | copy-start | bytes 196612
  167.5 10.4 %copy-start.5 = (f32[256,64]{1,0:T(8,128)S(1)}, f32[256,64]{1,0:T(8,128)}, u32[]{:S(2)}) copy-start(f32[256,64]{1,0:T(8,128)} %copy.43) | copy-start | bytes 196612
  197.2 29.9 %copy-start.3 = (f32[256,384]{1,0:T(8,128)S(1)}, f32[256,384]{1,0:T(8,128)}, u32[]{:S(2)}) copy-start(f32[256,384]{1,0:T(8,128)} %param.12) | copy-start | bytes 1179652
Sparse Core Ops, SparseCore 0:
  89.0 16.1 all-reduce.3
  209.0 16.1 all-reduce.5
where the time goes:
time: 260 us; the launch traced here: 259 us
  blocking collectives  93.9 us (36%)
  matrix products  58.3 us (22%)
  local copies, waits for them, and re-layouts  36 us (14%)
  waiting for transfers between devices  32.6 us (13%)
  between operations  18.6 us (7%)
  other arithmetic  12.3 us (5%)
  starting transfers between devices  7.36 us (3%)
    psum x2, blocking collectives, squares(): return lax.psum(jnp.sum(vector * vector), 'space')  40.1 us
    dot_general x2, matrix products, shards(): jnp.einsum('tpq,tdq->tdp', coeff, col_vals, precision=highest)  32.8 us
    psum x2, waiting for transfers between devices, shards(): pairs = lax.psum(owned, 'sub')  32.6 us
    psum x1, blocking collectives, shards(): alpha = norm_now / lax.psum(jnp.sum(direction * image), 'space')  22.2 us
    all_to_all x2, blocking collectives, shards(): lax.all_to_all(halo_terms, 'space', split_axis=0, concat_axis=0, tiled=True)  21.7 us
    dot_general x2, matrix products, shards(): jnp.einsum('tpq,tdp->tdq', coeff, row_vals, precision=highest)  20 us
    all_to_all x1, blocking collectives, shards(): lax.all_to_all(outgoing, 'space', split_axis=0, concat_axis=0, tiled=True)  9.88 us
    div x1, local copies, waits for them, and re-layouts, shards(): coupling / (gaps.astype(jnp.float32).reshape(tiles_here, BLOCK, BLOCK) +...  9.15 us
  transfers between devices with their start and end apart: 3, of which 2 were waited for; matrix products, arithmetic and copies ran while one was open for 9% of the time, Pallas kernels for 0%

commit v1 on v0

v1 whole, which is shorter than its diff:
```python
import functools

import jax
import jax.numpy as jnp
from jax import lax
from jax.experimental import pallas as pl
from jax.experimental.pallas import tpu as pltpu
from jax.sharding import PartitionSpec as P

BLOCK = 64
MODES = 6

coupling = 0.000244140625
gap_shift = 0.05

NN = (((1,), (0,)), ((), ()))
NT = (((1,), (1,)), ((), ()))
f32 = jnp.float32
bf16 = jnp.bfloat16


def pieces(x):
    hi = x.astype(bf16)
    rest = x - hi.astype(f32)
    mid = rest.astype(bf16)
    lo = (rest - mid.astype(f32)).astype(bf16)
    return hi, mid, lo


def dot3(x, onehot, dims):
    hi, mid, lo = [
        lax.dot_general(v, onehot, dims, preferred_element_type=f32) for v in pieces(x)
    ]
    return hi + (mid + lo)


def dot3_left(onehot, x, dims):
    hi, mid, lo = [
        lax.dot_general(onehot, v, dims, preferred_element_type=f32) for v in pieces(x)
    ]
    return hi + (mid + lo)


def total(x):
    return jnp.sum(jnp.sum(x, axis=0, keepdims=True), axis=1, keepdims=True)


def kernel(
    n, slots,
    force_ref, drag_ref, mode_ref, rows_ref, cols_ref, exports_ref, gaps_ref,
    vel_ref, res_ref,
    coeff, force_t, drag_t, oh_row, oh_col, oh_halo, oh_exp,
    row_t, col_t, u_row, u_col, image_t, second_t, dir_t, ret_t,
    pad, halo_t, own_send, own_recv,
    h_send, h_recv, t_send, t_recv, a_send, a_recv,
    h_ssem, h_rsem, t_ssem, t_rsem, o_ssem, o_rsem, a_ssem, a_rsem,
):
    me = lax.axis_index("space")
    sub = lax.axis_index("sub")
    other = 1 - sub
    tiles = coeff.shape[1]
    blocks = force_ref.shape[0]
    halo_pad = pad.shape[0]

    barrier = pltpu.get_barrier_semaphore()

    def greet(j, carry):
        peer = lax.rem(me + j, n)
        pl.semaphore_signal(
            barrier, inc=1, device_id={"space": peer, "sub": other},
            device_id_type=pl.DeviceIdType.MESH,
        )

        @pl.when(j > 0)
        def _():
            pl.semaphore_signal(
                barrier, inc=1, device_id={"space": peer, "sub": sub},
                device_id_type=pl.DeviceIdType.MESH,
            )

        return carry

    lax.fori_loop(0, n, greet, 0)

    def remote(src, dst, ssem, rsem, peer, core):
        return pltpu.make_async_remote_copy(
            src_ref=src, dst_ref=dst, send_sem=ssem, recv_sem=rsem,
            device_id={"space": peer, "sub": core},
            device_id_type=pl.DeviceIdType.MESH,
        )

    def peers(start, fn):
        def body(j, carry):
            fn(lax.rem(me + j, n))
            return carry

        lax.fori_loop(start, n, body, 0)

    def h_copy(i, peer, slot):
        return remote(
            h_send.at[i, peer], h_recv.at[i, slot], h_ssem.at[i, peer], h_rsem.at[i, slot],
            peer, sub,
        )

    def a_copy(i, peer, slot):
        return remote(
            a_send.at[i], a_recv.at[i, slot], a_ssem.at[i, peer], a_rsem.at[i, slot],
            peer, sub,
        )

    def t_same(i, peer, slot):
        return remote(
            t_send.at[i, peer], t_recv.at[i, sub, slot],
            t_ssem.at[i, 0, peer], t_rsem.at[i, sub, slot], peer, sub,
        )

    def t_cross(i, peer, slot, half):
        return remote(
            t_send.at[i, peer], t_recv.at[i, half, slot],
            t_ssem.at[i, 1, peer], t_rsem.at[i, half, slot], peer, other,
        )

    def own_copy(i):
        return remote(
            own_send.at[i], own_recv.at[i], o_ssem.at[i], o_rsem.at[i], me, other
        )

    def start_halo(i):
        for q in range(n):
            h_send[i, q] = pad[q * slots:(q + 1) * slots, :]
        h_recv[i, me] = h_send[i, me]

    def finish_halo(i):
        peers(1, lambda peer: h_copy(i, peer, peer).wait_recv())
        for q in range(n):
            pad[q * slots:(q + 1) * slots, :] = h_recv[i, q]

    pad[...] = jnp.zeros_like(pad)
    export_ids = exports_ref[...]
    oh_exp[...] = (
        export_ids == lax.broadcasted_iota(jnp.int32, (halo_pad, blocks), 1)
    ).astype(f32).astype(bf16)
    pad[...] = dot3_left(oh_exp[...], force_ref[...], NN)
    start_halo(0)
    pl.semaphore_wait(barrier, 2 * n - 1)
    peers(1, lambda peer: h_copy(0, peer, me).start())

    force_t[...] = jnp.transpose(force_ref[...])
    drag_t[...] = jnp.transpose(drag_ref[...])
    rows = rows_ref[...]
    cols = cols_ref[...]
    block_ids = lax.broadcasted_iota(jnp.int32, (blocks, tiles), 0)
    oh_row[...] = (rows == block_ids).astype(f32).astype(bf16)
    oh_col[...] = (cols == block_ids).astype(f32).astype(bf16)
    halo_ids = lax.broadcasted_iota(jnp.int32, (halo_pad, tiles), 0) + blocks
    oh_halo[...] = (cols == halo_ids).astype(f32).astype(bf16)
    chunk = 256
    eye = (
        lax.broadcasted_iota(jnp.int32, (chunk, chunk), 0)
        == lax.broadcasted_iota(jnp.int32, (chunk, chunk), 1)
    ).astype(f32).astype(bf16)

    def prepare(j, carry):
        at = pl.ds(pl.multiple_of(j * chunk, chunk), chunk)
        turned = lax.dot_general(eye, gaps_ref[:, at], NT, preferred_element_type=f32)
        coeff[at, :] = coupling / (turned + gap_shift)
        return carry

    lax.fori_loop(0, coeff.shape[0] // chunk, prepare, 0)

    lanes = 128
    groups = tiles // lanes
    pairs_of_modes = MODES // 2

    def apply_tiles(vec):
        row_t[...] = dot3(vec, oh_row[...], NN)
        col_t[...] = dot3(vec, oh_col[...], NN) + dot3(halo_t[...], oh_halo[...], NN)

        def outer(g, carry):
            lane = pl.ds(pl.multiple_of(lax.rem(g, groups) * lanes, lanes), lanes)
            base = (g // groups) * (2 * BLOCK)
            first = pl.ds(pl.multiple_of(base, BLOCK), BLOCK)
            second = pl.ds(pl.multiple_of(base + BLOCK, BLOCK), BLOCK)
            col_a = col_t[first, lane]
            col_b = col_t[second, lane]

            def inner(i, accs):
                acc_a, acc_b = accs
                at_a = pl.ds(pl.multiple_of(base + i * 8, 8), 8)
                at_b = pl.ds(pl.multiple_of(base + BLOCK + i * 8, 8), 8)
                rows_a = row_t[at_a, lane]
                rows_b = row_t[at_b, lane]
                out_a, out_b = [], []
                for k in range(8):
                    c = coeff[pl.ds(pl.multiple_of((i * 8 + k) * BLOCK, BLOCK), BLOCK), lane]
                    w_a = c * (rows_a[k:k + 1, :] - col_a)
                    w_b = c * (rows_b[k:k + 1, :] - col_b)
                    acc_a = acc_a - w_a
                    acc_b = acc_b - w_b
                    out_a.append(jnp.sum(w_a, axis=0, keepdims=True))
                    out_b.append(jnp.sum(w_b, axis=0, keepdims=True))
                u_row[at_a, lane] = jnp.concatenate(out_a, axis=0)
                u_row[at_b, lane] = jnp.concatenate(out_b, axis=0)
                return acc_a, acc_b

            zero = jnp.zeros((BLOCK, lanes), f32)
            acc_a, acc_b = lax.fori_loop(0, BLOCK // 8, inner, (zero, zero))
            u_col[first, lane] = acc_a
            u_col[second, lane] = acc_b
            return carry

        lax.fori_loop(0, groups * pairs_of_modes, outer, 0)

    def send_terms(i):
        halo_terms = dot3(u_col[...], oh_halo[...], NT)
        pad[...] = jnp.transpose(halo_terms)
        for q in range(n):
            t_send[i, q] = pad[q * slots:(q + 1) * slots, :]
        t_recv[i, sub, me] = t_send[i, me]

        def push(peer):
            t_cross(i, peer, me, sub).start()

            @pl.when(peer != me)
            def _():
                t_same(i, peer, me).start()

        peers(0, push)
        own_send[i] = dot3(u_row[...], oh_row[...], NT) + dot3(u_col[...], oh_col[...], NT)
        own_copy(i).start()

    def collect_terms(i):
        def pull(peer):
            t_cross(i, peer, peer, other).wait_recv()

            @pl.when(peer != me)
            def _():
                t_same(i, peer, peer).wait_recv()

        peers(0, pull)
        for q in range(n):
            pad[q * slots:(q + 1) * slots, :] = t_recv[i, 0, q] + t_recv[i, 1, q]
        ret_t[...] = dot3(jnp.transpose(pad[...]), oh_exp[...], NN)
        own_copy(i).wait_recv()

    def operator_rows(i, at, vec_ref):
        spans = [pl.ds(pl.multiple_of(c * BLOCK + at * 8, 8), 8) for c in range(MODES)]
        pair = [
            (own_send[i, span, :] + own_recv[i, span, :]) + ret_t[span, :] for span in spans
        ]
        out = []
        for c in range(MODES):
            mixed = mode_ref[c, 0] * pair[0]
            for k in range(1, MODES):
                mixed = mixed + mode_ref[c, k] * pair[k]
            out.append(drag_t[spans[c], :] * vec_ref[spans[c], :] + mixed)
        return spans, out

    def fold(x):
        acc = x[:, :128]
        for k in range(1, blocks // 128):
            acc = acc + x[:, k * 128:(k + 1) * 128]
        return acc

    def share(i):
        a_recv[i, me] = a_send[i]
        peers(1, lambda peer: a_copy(i, peer, me).start())

    def gather_sums(i):
        peers(1, lambda peer: a_copy(i, peer, peer).wait_recv())
        acc = a_recv[i, 0]
        for q in range(1, n):
            acc = acc + a_recv[i, q]
        return acc

    finish_halo(0)
    halo_t[...] = jnp.transpose(pad[...])
    apply_tiles(force_t[...])
    send_terms(0)
    collect_terms(0)

    def first_image(at, sums):
        norm, dots = sums
        spans, out = operator_rows(0, at, force_t)
        for c in range(MODES):
            v = force_t[spans[c], :]
            image_t[spans[c], :] = out[c]
            norm = norm + v * v
            dots = dots + v * out[c]
        return norm, dots

    zero = jnp.zeros((8, blocks), f32)
    norm, dots = lax.fori_loop(0, BLOCK // 8, first_image, (zero, zero))
    a_send[0, 0:8, :] = fold(norm)
    a_send[0, 8:16, :] = fold(dots)
    share(0)
    pad[...] = dot3_left(oh_exp[...], image_t[...], NT)
    start_halo(1)
    peers(1, lambda peer: h_copy(1, peer, me).start())
    finish_halo(1)
    sums = gather_sums(0)
    norm0 = total(sums[0:8, :])
    alpha0 = norm0 / total(sums[8:16, :])
    halo_t[...] = halo_t[...] - alpha0 * jnp.transpose(pad[...])
    second_t[...] = force_t[...] - alpha0 * image_t[...]
    resid = second_t[...]
    squares = resid * resid
    part = squares[0:8, :]
    for k in range(1, MODES * BLOCK // 8):
        part = part + squares[k * 8:(k + 1) * 8, :]
    a_send[1, 0:8, :] = fold(part)
    a_send[1, 8:16, :] = jnp.zeros((8, 128), f32)
    share(1)

    apply_tiles(second_t[...])
    send_terms(1)
    norm1 = total(gather_sums(1)[0:8, :])
    beta = norm1 / norm0
    collect_terms(1)

    def second_image(at, dots):
        spans, out = operator_rows(1, at, second_t)
        for c in range(MODES):
            image = out[c] + beta * image_t[spans[c], :]
            direction = second_t[spans[c], :] + beta * force_t[spans[c], :]
            image_t[spans[c], :] = image
            dir_t[spans[c], :] = direction
            dots = dots + direction * image
        return dots

    dots = lax.fori_loop(0, BLOCK // 8, second_image, zero)
    a_send[2, 0:8, :] = fold(dots)
    a_send[2, 8:16, :] = jnp.zeros((8, 128), f32)
    share(2)
    alpha1 = norm1 / total(gather_sums(2)[0:8, :])
    vel_ref[...] = jnp.transpose(alpha0 * force_t[...] + alpha1 * dir_t[...])
    res_ref[...] = jnp.transpose(second_t[...] - alpha1 * image_t[...])

    for i in range(2):
        peers(1, lambda peer: h_copy(i, peer, me).wait_send())
        peers(1, lambda peer: t_same(i, peer, me).wait_send())
        peers(0, lambda peer: t_cross(i, peer, me, sub).wait_send())
        own_copy(i).wait_send()
    for i in range(3):
        peers(1, lambda peer: a_copy(i, peer, me).wait_send())


def shards(n, force, drag, mode_matrix, tile_rows, tile_cols, gaps, send_blocks):
    blocks, width = force.shape
    tiles = tile_rows.shape[0]
    slots = send_blocks.shape[2]
    halo = n * slots
    halo_pad = -(-halo // 128) * 128
    exports = jnp.full((halo_pad, 1), -1, jnp.int32).at[:halo, 0].set(send_blocks.reshape(halo))
    vmem = pl.BlockSpec(memory_space=pltpu.VMEM)
    wide = lambda *shape: pltpu.VMEM(shape, f32)
    out = jax.ShapeDtypeStruct((blocks, width), f32)
    return pl.pallas_call(
        functools.partial(kernel, n, slots),
        out_shape=(out, out),
        in_specs=[vmem, vmem, pl.BlockSpec(memory_space=pltpu.SMEM), vmem, vmem, vmem, vmem],
        out_specs=(vmem, vmem),
        scratch_shapes=[
            wide(gaps.shape[1], tiles),
            wide(width, blocks), wide(width, blocks),
            pltpu.VMEM((blocks, tiles), bf16), pltpu.VMEM((blocks, tiles), bf16),
            pltpu.VMEM((halo_pad, tiles), bf16), pltpu.VMEM((halo_pad, blocks), bf16),
            wide(width, tiles), wide(width, tiles), wide(width, tiles), wide(width, tiles),
            wide(width, blocks), wide(width, blocks), wide(width, blocks), wide(width, blocks),
            wide(halo_pad, width), wide(width, halo_pad),
            wide(2, width, blocks), wide(2, width, blocks),
            wide(2, n, slots, width), wide(2, n, slots, width),
            wide(2, n, slots, width), wide(2, 2, n, slots, width),
            wide(3, 16, 128), wide(3, n, 16, 128),
            pltpu.SemaphoreType.DMA((2, n)), pltpu.SemaphoreType.DMA((2, n)),
            pltpu.SemaphoreType.DMA((2, 2, n)), pltpu.SemaphoreType.DMA((2, 2, n)),
            pltpu.SemaphoreType.DMA((2,)), pltpu.SemaphoreType.DMA((2,)),
            pltpu.SemaphoreType.DMA((3, n)), pltpu.SemaphoreType.DMA((3, n)),
        ],
        compiler_params=pltpu.CompilerParams(
            collective_id=0, has_side_effects=True, vmem_limit_bytes=48 * 1024 * 1024
        ),
    )(
        force, drag, mode_matrix, tile_rows.reshape(1, tiles), tile_cols.reshape(1, tiles),
        exports, gaps,
    )


def solution(mesh):
    return jax.shard_map(
        functools.partial(shards, mesh.shape["space"]),
        mesh=mesh,
        in_specs=(
            P(("real", "space"), None),
            P(("real", "space"), None),
            P(),
            P(("real", "space", "sub")),
            P(("real", "space", "sub")),
            P(("real", "space", "sub"), None),
            P(("real", "space"), None, None),
        ),
        out_specs=(P(("real", "space"), None), P(("real", "space"), None)),
        check_vma=False,
    )
```

time: 260 us -> 54.3 us (0.21)
  blocking collectives: 93.9 us -> 0 us
  matrix products: 58.3 us -> 0 us
  Pallas kernels: 0 us -> 45.4 us
  waiting for transfers between devices: 32.6 us -> 0 us
  local copies, waits for them, and re-layouts: 36 us -> 7.96 us
  between operations: 18.6 us -> 0.65 us
  other arithmetic: 12.3 us -> 0 us
  starting transfers between devices: 7.36 us -> 0 us
    psum x3 -> x0, blocking collectives: 62.3 us -> none  [the longest x2 40.1 us: squares(): return lax.psum(jnp.sum(vector * vector), 'space')]
    dot_general x12 -> x0, matrix products: 58.3 us -> none  [the longest x2 32.8 us: shards(): jnp.einsum('tpq,tdq->tdp', coeff, col_vals, precision=highest)]
    pallas_call x0 -> x1, Pallas kernels: none -> 45.4 us  [shards(): pl.pallas_call(functools.partial(kernel, n, slots), out_shape=(out, out),...]
    psum x2 -> x0, waiting for transfers between devices: 32.6 us -> none  [shards(): pairs = lax.psum(owned, 'sub')]
    all_to_all x3 -> x0, blocking collectives: 31.6 us -> none  [the longest x2 21.7 us: shards(): lax.all_to_all(halo_terms, 'space', split_axis=0, concat_axis=0, tiled=True)]
    div x1 -> x0, local copies, waits for them, and re-layouts: 9.15 us -> none  [shards(): coupling / (gaps.astype(jnp.float32).reshape(tiles_here, BLOCK, BLOCK) +...]
    all_to_all x1 -> x0, starting transfers between devices: 7.28 us -> none  [shards(): lax.all_to_all(outgoing, 'space', split_axis=0, concat_axis=0, tiled=True)]
    gather x6 -> x0, local copies, waits for them, and re-layouts: 6.42 us -> none  [the longest x2 2.34 us: shards(): jnp.take(direction, exports, axis=0).reshape(nspace, slots, width)]
  transfers between devices with their start and end apart: 3 -> 0, of which waited for: 2 -> 0; matrix products, arithmetic and copies ran while one was open for 9% -> 0% of each run, Pallas kernels for 0% -> 0%
where the time goes in v1:
time: 54.3 us; the launch traced here: 54 us
  Pallas kernels  45.4 us (84%)
  local copies, waits for them, and re-layouts  7.96 us (15%)
  between operations  0.65 us (1%)
    pallas_call x1, Pallas kernels, shards(): pl.pallas_call(functools.partial(kernel, n, slots), out_shape=(out, out),...  45.4 us
    unnamed x15, local copies, waits for them, and re-layouts  7.88 us

profile of v1, /device:TPU:0, one launch (start us, length us, event | category | flops | bytes accessed | tf_op | source)
XLA Modules:
  0.0 54.0 jit_solution(18201748199654585543)
XLA Ops:
  0.6 0.8 %copy.11 = s32[1,8,4]{2,1,0:T(8,128)S(1)} copy(s32[1,8,4]{1,2,0:T(4,128)} %param.15) | data formatting | bytes 256 | tf_op args[6]
  1.4 0.1 reshape.46
  1.5 0.0 copy-start
  1.5 1.6 %copy-done = bf16[256,4096]{1,0:T(8,128)(2,1)S(1)} copy-done((bf16[256,4096]{1,0:T(8,128)(2,1)S(1)}, bf16[256,4096]{1,0:T(8,128)(2,1)}, u32[]{:S(2)}) %copy-start) | copy-done | bytes 2097176
  3.1 0.0 copy-start.1
  3.1 1.0 %copy-done.1 = f32[256,384]{1,0:T(8,128)S(1)} copy-done((f32[256,384]{1,0:T(8,128)S(1)}, f32[256,384]{1,0:T(8,128)}, u32[]{:S(2)}) %copy-start.1) | copy-done | bytes 393240
  4.1 0.0 copy-start.2
  4.1 1.0 %copy-done.2 = f32[256,384]{1,0:T(8,128)S(1)} copy-done((f32[256,384]{1,0:T(8,128)S(1)}, f32[256,384]{1,0:T(8,128)}, u32[]{:S(2)}) %copy-start.2) | copy-done | bytes 393240
  5.1 0.0 copy-start.3
  5.1 0.7 %copy-done.3 = f32[6,6]{1,0:T(8,128)S(1)} copy-done((f32[6,6]{1,0:T(8,128)S(1)}, f32[6,6]{1,0:T(8,128)}, u32[]{:S(2)}) %copy-start.3) | copy-done | bytes 168
  5.7 0.0 copy-start.4
  5.7 0.7 %copy-done.4 = s32[256]{0:T(256)S(1)} copy-done((s32[256]{0:T(256)S(1)}, s32[256]{0:T(256)}, u32[]{:S(2)}) %copy-start.4) | copy-done | bytes 1048
  6.4 0.0 copy-start.5
  6.4 0.7 %copy-done.5 = s32[256]{0:T(256)S(1)} copy-done((s32[256]{0:T(256)S(1)}, s32[256]{0:T(256)}, u32[]{:S(2)}) %copy-start.5) | copy-done | bytes 1048
  7.1 45.4 %shard_map.86 = (f32[256,384]{1,0:T(8,128)S(1)}, f32[256,384]{1,0:T(8,128)S(1)}) custom-call(f32[256,384]{1,0:T(8,128)S(1)} %copy-done.1, f32[256,384]{1,0:T(8,128)S(1)} %copy-done.2, f32[6,6]{1,0:T(8,128)S(1)} %copy-done.3, s32[1,256]{1,0:T(1,128)S(1)} %bitcast.2, s32[1,256]{1,0:T(1,128)S(1)} %bitcast.3, s32[128,1]{1,0:T(8,128)S(1)} %scatter.4.exports_ref, ...), custom_call_target="tpu_custom_call" | custom-call | tf_op jit(solution)/shard_map/pallas_call | solution.py:358
  52.5 0.7 %copy.15 = f32[256,384]{1,0:T(8,128)} copy(f32[256,384]{1,0:T(8,128)S(1)} %get-tuple-element.16) | data formatting | bytes 786432
  53.3 0.7 %copy.16 = f32[256,384]{1,0:T(8,128)} copy(f32[256,384]{1,0:T(8,128)S(1)} %get-tuple-element.17) | data formatting | bytes 786432
  (1 shorter events, 0.0 us)
Async XLA Ops:
  1.5 1.6 %copy-start = (bf16[256,4096]{1,0:T(8,128)(2,1)S(1)}, bf16[256,4096]{1,0:T(8,128)(2,1)}, u32[]{:S(2)}) copy-start(bf16[256,4096]{1,0:T(8,128)(2,1)} %gaps_ref.1) | copy-start | bytes 6291460
  3.1 1.0 %copy-start.1 = (f32[256,384]{1,0:T(8,128)S(1)}, f32[256,384]{1,0:T(8,128)}, u32[]{:S(2)}) copy-start(f32[256,384]{1,0:T(8,128)} %force_ref.1) | copy-start | bytes 1179652
  4.1 1.0 %copy-start.2 = (f32[256,384]{1,0:T(8,128)S(1)}, f32[256,384]{1,0:T(8,128)}, u32[]{:S(2)}) copy-start(f32[256,384]{1,0:T(8,128)} %drag_ref.1) | copy-start | bytes 1179652
  5.1 0.7 %copy-start.3 = (f32[6,6]{1,0:T(8,128)S(1)}, f32[6,6]{1,0:T(8,128)}, u32[]{:S(2)}) copy-start(f32[6,6]{1,0:T(8,128)} %mode_ref.1) | copy-start | bytes 436
  5.7 0.7 %copy-start.4 = (s32[256]{0:T(256)S(1)}, s32[256]{0:T(256)}, u32[]{:S(2)}) copy-start(s32[256]{0:T(256)} %param.12) | copy-start | bytes 3076
  6.4 0.7 %copy-start.5 = (s32[256]{0:T(256)S(1)}, s32[256]{0:T(256)}, u32[]{:S(2)}) copy-start(s32[256]{0:T(256)} %param.13) | copy-start | bytes 3076

commit v2 on v1

--- a/solution.py
+++ b/solution.py
@@ -47,14 +47,24 @@
 
 def kernel(
     n, slots,
-    force_ref, drag_ref, mode_ref, rows_ref, cols_ref, exports_ref, gaps_ref,
+    force_hbm, drag_hbm, mode_ref, rows_hbm, cols_hbm, exports_ref, gaps_hbm,
     vel_ref, res_ref,
     coeff, force_t, drag_t, oh_row, oh_col, oh_halo, oh_exp,
     row_t, col_t, u_row, u_col, image_t, second_t, dir_t, ret_t,
     pad, halo_t, own_send, own_recv,
     h_send, h_recv, t_send, t_recv, a_send, a_recv,
     h_ssem, h_rsem, t_ssem, t_rsem, o_ssem, o_rsem, a_ssem, a_rsem,
+    force_ref, drag_ref, rows_ref, cols_ref, gaps_ref, in_sem,
 ):
+    loads = [
+        pltpu.make_async_copy(src, dst, in_sem.at[k])
+        for k, (src, dst) in enumerate((
+            (force_hbm, force_ref), (rows_hbm, rows_ref), (cols_hbm, cols_ref),
+            (gaps_hbm, gaps_ref), (drag_hbm, drag_ref),
+        ))
+    ]
+    for load in loads:
+        load.start()
     me = lax.axis_index("space")
     sub = lax.axis_index("sub")
     other = 1 - sub
@@ -140,11 +150,14 @@
     oh_exp[...] = (
         export_ids == lax.broadcasted_iota(jnp.int32, (halo_pad, blocks), 1)
     ).astype(f32).astype(bf16)
+    loads[0].wait()
     pad[...] = dot3_left(oh_exp[...], force_ref[...], NN)
     start_halo(0)
     pl.semaphore_wait(barrier, 2 * n - 1)
     peers(1, lambda peer: h_copy(0, peer, me).start())
 
+    for load in loads[1:]:
+        load.wait()
     force_t[...] = jnp.transpose(force_ref[...])
     drag_t[...] = jnp.transpose(drag_ref[...])
     rows = rows_ref[...]
@@ -353,12 +366,13 @@
     halo_pad = -(-halo // 128) * 128
     exports = jnp.full((halo_pad, 1), -1, jnp.int32).at[:halo, 0].set(send_blocks.reshape(halo))
     vmem = pl.BlockSpec(memory_space=pltpu.VMEM)
+    hbm = pl.BlockSpec(memory_space=pl.ANY)
     wide = lambda *shape: pltpu.VMEM(shape, f32)
     out = jax.ShapeDtypeStruct((blocks, width), f32)
     return pl.pallas_call(
         functools.partial(kernel, n, slots),
         out_shape=(out, out),
-        in_specs=[vmem, vmem, pl.BlockSpec(memory_space=pltpu.SMEM), vmem, vmem, vmem, vmem],
+        in_specs=[hbm, hbm, pl.BlockSpec(memory_space=pltpu.SMEM), hbm, hbm, vmem, hbm],
         out_specs=(vmem, vmem),
         scratch_shapes=[
             wide(gaps.shape[1], tiles),
@@ -376,9 +390,12 @@
             pltpu.SemaphoreType.DMA((2, 2, n)), pltpu.SemaphoreType.DMA((2, 2, n)),
             pltpu.SemaphoreType.DMA((2,)), pltpu.SemaphoreType.DMA((2,)),
             pltpu.SemaphoreType.DMA((3, n)), pltpu.SemaphoreType.DMA((3, n)),
+            wide(blocks, width), wide(blocks, width),
+            pltpu.VMEM((1, tiles), jnp.int32), pltpu.VMEM((1, tiles), jnp.int32),
+            pltpu.VMEM(gaps.shape, gaps.dtype), pltpu.SemaphoreType.DMA((5,)),
         ],
         compiler_params=pltpu.CompilerParams(
-            collective_id=0, has_side_effects=True, vmem_limit_bytes=48 * 1024 * 1024
+            collective_id=0, has_side_effects=True, vmem_limit_bytes=63 * 1024 * 1024
         ),
     )(
         force, drag, mode_matrix, tile_rows.reshape(1, tiles), tile_cols.reshape(1, tiles),

time: 54.3 us -> 52.6 us (0.969)
  local copies, waits for them, and re-layouts: 7.96 us -> 5 us
  Pallas kernels: 45.4 us -> 46.6 us
    unnamed x15 -> x3, local copies, waits for them, and re-layouts: 7.88 us -> 4.29 us
    pallas_call x1, Pallas kernels: 45.4 us -> 46.6 us  [shards(): pl.pallas_call(functools.partial(kernel, n, slots), out_shape=(out, out),...]
    scatter x1, local copies, waits for them, and re-layouts: 0.01 us -> 0.64 us  [shards(): jnp.full((halo_pad, 1), -1, jnp.int32).at[:halo, 0]]
where the time goes in v2:
time: 52.6 us; the launch traced here: 52.3 us
  Pallas kernels  46.6 us (89%)
  local copies, waits for them, and re-layouts  5 us (10%)
  between operations  0.64 us (1%)
    pallas_call x1, Pallas kernels, shards(): pl.pallas_call(functools.partial(kernel, n, slots), out_shape=(out, out),...  46.6 us
    unnamed x3, local copies, waits for them, and re-layouts  4.29 us

profile of v2, /device:TPU:0, one launch (start us, length us, event | category | flops | bytes accessed | tf_op | source)
XLA Modules:
  0.0 52.3 jit_solution(16068858356640753073)
XLA Ops:
  0.6 0.8 %copy.11 = s32[1,8,4]{2,1,0:T(8,128)S(1)} copy(s32[1,8,4]{1,2,0:T(4,128)} %param.15) | data formatting | bytes 256 | tf_op args[6]
  1.4 0.1 reshape.46
  1.5 0.6 %scatter.4.exports_ref = s32[128,1]{1,0:T(8,128)} pad(s32[32,1]{1,0:T(8,128)S(1)} %reshape.46, s32[]{:T(128)} %constant.27.clone.1), padding=0_96x0_0 | pad | bytes 644 | tf_op jit(solution)/shard_map/scatter | solution.py:367
  2.1 46.6 %shard_map.86 = (f32[256,384]{1,0:T(8,128)}, f32[256,384]{1,0:T(8,128)}) custom-call(f32[256,384]{1,0:T(8,128)} %force_hbm.1, f32[256,384]{1,0:T(8,128)} %drag_hbm.1, f32[6,6]{1,0:T(8,128)} %mode_ref.1, s32[1,256]{1,0:T(1,128)} %bitcast.2, s32[1,256]{1,0:T(1,128)} %bitcast.3, s32[128,1]{1,0:T(8,128)} %scatter.4.exports_ref, bf16[256,4096]{1,0:T(8,128)(2,1)} %gaps_hbm.1), custom_call_target="tpu_custom_call" | custom-call | tf_op jit(solution)/shard_map/pallas_call | solution.py:372
  48.7 1.8 %copy.15 = f32[256,384]{1,0:T(8,128)} copy(f32[256,384]{1,0:T(8,128)} %get-tuple-element.16) | data formatting | bytes 786432
  50.5 1.8 %copy.16 = f32[256,384]{1,0:T(8,128)} copy(f32[256,384]{1,0:T(8,128)} %get-tuple-element.17) | data formatting | bytes 786432

commit v3 on v2

--- a/solution.py
+++ b/solution.py
@@ -54,7 +54,7 @@
     pad, halo_t, own_send, own_recv,
     h_send, h_recv, t_send, t_recv, a_send, a_recv,
     h_ssem, h_rsem, t_ssem, t_rsem, o_ssem, o_rsem, a_ssem, a_rsem,
-    force_ref, drag_ref, rows_ref, cols_ref, gaps_ref, in_sem,
+    force_ref, drag_ref, rows_ref, cols_ref, gaps_ref, in_sem, oh_wide,
 ):
     loads = [
         pltpu.make_async_copy(src, dst, in_sem.at[k])
@@ -146,10 +146,13 @@
             pad[q * slots:(q + 1) * slots, :] = h_recv[i, q]
 
     pad[...] = jnp.zeros_like(pad)
-    export_ids = exports_ref[...]
-    oh_exp[...] = (
-        export_ids == lax.broadcasted_iota(jnp.int32, (halo_pad, blocks), 1)
-    ).astype(f32).astype(bf16)
+    oh_wide[...] = jnp.zeros_like(oh_wide)
+    lane_ids = lax.broadcasted_iota(jnp.int32, (1, blocks), 1)
+    for q in range(n):
+        for k in range(slots):
+            at = q * slots + k
+            oh_wide[at:at + 1, :] = (lane_ids == exports_ref[0, q, k]).astype(f32)
+    oh_exp[...] = oh_wide[...].astype(bf16)
     loads[0].wait()
     pad[...] = dot3_left(oh_exp[...], force_ref[...], NN)
     start_halo(0)
@@ -364,15 +367,15 @@
     slots = send_blocks.shape[2]
     halo = n * slots
     halo_pad = -(-halo // 128) * 128
-    exports = jnp.full((halo_pad, 1), -1, jnp.int32).at[:halo, 0].set(send_blocks.reshape(halo))
+    smem = pl.BlockSpec(memory_space=pltpu.SMEM)
     vmem = pl.BlockSpec(memory_space=pltpu.VMEM)
     hbm = pl.BlockSpec(memory_space=pl.ANY)
     wide = lambda *shape: pltpu.VMEM(shape, f32)
-    out = jax.ShapeDtypeStruct((blocks, width), f32)
+    out = pltpu.VMEM((blocks, width), f32)
     return pl.pallas_call(
         functools.partial(kernel, n, slots),
         out_shape=(out, out),
-        in_specs=[hbm, hbm, pl.BlockSpec(memory_space=pltpu.SMEM), hbm, hbm, vmem, hbm],
+        in_specs=[hbm, hbm, smem, hbm, hbm, smem, hbm],
         out_specs=(vmem, vmem),
         scratch_shapes=[
             wide(gaps.shape[1], tiles),
@@ -393,13 +396,14 @@
             wide(blocks, width), wide(blocks, width),
             pltpu.VMEM((1, tiles), jnp.int32), pltpu.VMEM((1, tiles), jnp.int32),
             pltpu.VMEM(gaps.shape, gaps.dtype), pltpu.SemaphoreType.DMA((5,)),
+            wide(halo_pad, blocks),
         ],
         compiler_params=pltpu.CompilerParams(
             collective_id=0, has_side_effects=True, vmem_limit_bytes=63 * 1024 * 1024
         ),
     )(
         force, drag, mode_matrix, tile_rows.reshape(1, tiles), tile_cols.reshape(1, tiles),
-        exports, gaps,
+        send_blocks, gaps,
     )
 
 

time: 52.6 us -> 49.4 us (0.939)
  local copies, waits for them, and re-layouts: 5 us -> 2.84 us
  Pallas kernels: 46.6 us -> 45.7 us
    unnamed x3, local copies, waits for them, and re-layouts: 4.29 us -> 2.84 us
    pallas_call x1, Pallas kernels: 46.6 us -> 45.7 us  [shards(): pl.pallas_call(functools.partial(kernel, n, slots), out_shape=(out, out),...]
    scatter x1 -> x0, local copies, waits for them, and re-layouts: 0.64 us -> none  [shards(): jnp.full((halo_pad, 1), -1, jnp.int32).at[:halo, 0]]
where the time goes in v3:
time: 49.4 us; the launch traced here: 49.2 us
  Pallas kernels  45.7 us (93%)
  local copies, waits for them, and re-layouts  2.84 us (6%)
  between operations  0.64 us (1%)
    pallas_call x1, Pallas kernels, shards(): pl.pallas_call(functools.partial(kernel, n, slots), out_shape=(out, out),...  45.7 us
    unnamed x3, local copies, waits for them, and re-layouts  2.84 us

profile of v3, /device:TPU:0, one launch (start us, length us, event | category | flops | bytes accessed | tf_op | source)
XLA Modules:
  0.0 49.2 jit_solution(13762130805009954429)
XLA Ops:
  0.6 1.3 %copy.9.exports_ref = s32[1,8,4]{2,1,0:T(8,128)} copy(s32[1,8,4]{1,2,0:T(4,128)} %param.13) | data formatting | bytes 256 | tf_op args[6]
  2.0 45.7 %shard_map.86 = (f32[256,384]{1,0:T(8,128)S(1)}, f32[256,384]{1,0:T(8,128)S(1)}) custom-call(f32[256,384]{1,0:T(8,128)} %force_hbm.1, f32[256,384]{1,0:T(8,128)} %drag_hbm.1, f32[6,6]{1,0:T(8,128)} %mode_ref.1, s32[1,256]{1,0:T(1,128)} %bitcast.2, s32[1,256]{1,0:T(1,128)} %bitcast.3, s32[1,8,4]{2,1,0:T(8,128)} %copy.9.exports_ref, bf16[256,4096]{1,0:T(8,128)(2,1)} %gaps_hbm.1), custom_call_target="tpu_custom_call" | custom-call | tf_op jit(solution)/shard_map/pallas_call | solution.py:375
  47.7 0.7 %copy.12 = f32[256,384]{1,0:T(8,128)} copy(f32[256,384]{1,0:T(8,128)S(1)} %get-tuple-element.2) | data formatting | bytes 786432
  48.4 0.7 %copy.13 = f32[256,384]{1,0:T(8,128)} copy(f32[256,384]{1,0:T(8,128)S(1)} %get-tuple-element.3) | data formatting | bytes 786432

commit v4 on v3

--- a/solution.py
+++ b/solution.py
@@ -39,6 +39,29 @@
         lax.dot_general(onehot, v, dims, preferred_element_type=f32) for v in pieces(x)
     ]
     return hi + (mid + lo)
+
+
+def fold_rows(w):
+    parts = [w[k:k + 8, :] for k in range(0, w.shape[0], 8)]
+    while len(parts) > 1:
+        parts = [a + b for a, b in zip(parts[::2], parts[1::2])]
+    return parts[0]
+
+
+def row_totals(xs):
+    row = lax.broadcasted_iota(jnp.int32, xs[0].shape, 0)
+    low = row < 4
+    ys = [
+        jnp.where(low, a, b) + pltpu.roll(jnp.where(low, b, a), 4, 0)
+        for a, b in zip(xs[:4], xs[4:])
+    ]
+    for step in (2, 1):
+        keep = row % (2 * step) < step
+        ys = [
+            jnp.where(keep, a + pltpu.roll(a, 8 - step, 0), b + pltpu.roll(b, step, 0))
+            for a, b in zip(ys[:step], ys[step:])
+        ]
+    return ys[0]
 
 
 def total(x):
@@ -213,10 +236,10 @@
                     w_b = c * (rows_b[k:k + 1, :] - col_b)
                     acc_a = acc_a - w_a
                     acc_b = acc_b - w_b
-                    out_a.append(jnp.sum(w_a, axis=0, keepdims=True))
-                    out_b.append(jnp.sum(w_b, axis=0, keepdims=True))
-                u_row[at_a, lane] = jnp.concatenate(out_a, axis=0)
-                u_row[at_b, lane] = jnp.concatenate(out_b, axis=0)
+                    out_a.append(fold_rows(w_a))
+                    out_b.append(fold_rows(w_b))
+                u_row[at_a, lane] = row_totals(out_a)
+                u_row[at_b, lane] = row_totals(out_b)
                 return acc_a, acc_b
 
             zero = jnp.zeros((BLOCK, lanes), f32)

time: 49.4 us -> 48.8 us (0.988)
  Pallas kernels: 45.7 us -> 45 us
    pallas_call x1, Pallas kernels: 45.7 us -> 45 us  [shards(): pl.pallas_call(functools.partial(kernel, n, slots), out_shape=(out, out),...]
where the time goes in v4:
time: 48.8 us; the launch traced here: 48.5 us
  Pallas kernels  45 us (92%)
  local copies, waits for them, and re-layouts  2.84 us (6%)
  between operations  0.64 us (1%)
    pallas_call x1, Pallas kernels, shards(): pl.pallas_call(functools.partial(kernel, n, slots), out_shape=(out, out),...  45 us
    unnamed x3, local copies, waits for them, and re-layouts  2.84 us

profile of v4, /device:TPU:0, one launch (start us, length us, event | category | flops | bytes accessed | tf_op | source)
XLA Modules:
  0.0 48.5 jit_solution(14977613875874466146)
XLA Ops:
  0.6 1.3 %copy.9.exports_ref = s32[1,8,4]{2,1,0:T(8,128)} copy(s32[1,8,4]{1,2,0:T(4,128)} %param.13) | data formatting | bytes 256 | tf_op args[6]
  2.0 45.0 %shard_map.86 = (f32[256,384]{1,0:T(8,128)S(1)}, f32[256,384]{1,0:T(8,128)S(1)}) custom-call(f32[256,384]{1,0:T(8,128)} %force_hbm.1, f32[256,384]{1,0:T(8,128)} %drag_hbm.1, f32[6,6]{1,0:T(8,128)} %mode_ref.1, s32[1,256]{1,0:T(1,128)} %bitcast.2, s32[1,256]{1,0:T(1,128)} %bitcast.3, s32[1,8,4]{2,1,0:T(8,128)} %copy.9.exports_ref, bf16[256,4096]{1,0:T(8,128)(2,1)} %gaps_hbm.1), custom_call_target="tpu_custom_call" | custom-call | tf_op jit(solution)/shard_map/pallas_call | solution.py:398
  47.0 0.7 %copy.12 = f32[256,384]{1,0:T(8,128)} copy(f32[256,384]{1,0:T(8,128)S(1)} %get-tuple-element.2) | data formatting | bytes 786432
  47.8 0.7 %copy.13 = f32[256,384]{1,0:T(8,128)} copy(f32[256,384]{1,0:T(8,128)S(1)} %get-tuple-element.3) | data formatting | bytes 786432
